TPU v7x, 32 devices: a whole 2x2x4 slice. The times are simulated.
32 devices in a mesh: cuts: 4 (over x, core), tile: 8 (over z, y).
Axes of the slice: x: 2, y: 2, z: 4, core: 2. Of those that a mesh axis runs over, the one named last changes fastest.
Arguments:
- state_in: float32 [4, 2, 128, 1024], P('cuts', None, 'tile'), may hold values from -0.625 to 0.625
- sea_depth: float32 [128, 1024], P('tile'), may hold values from 1.5 to 3
- pressure: float32 [128, 1024], P('tile'), may hold values from -3 to 3
Outputs:
- state_out: float32 [4, 2, 128, 1024], P('cuts', None, 'tile')
All inputs are finite; a program needn't handle non-finite values.
Results may differ from a plain program's by a relative error of at most 0.0003.
Values sent between devices are 32-bit elements; how exact they have to be, the bound alone decides.
A program may use at most 64 MiB of HBM per device.

v0:
```python
import functools
import math

import jax
import jax.numpy as jnp
from jax import lax
from jax.experimental import pallas as pl
from jax.experimental.pallas import tpu as pltpu
from jax.sharding import PartitionSpec as P

LEVELS = 8
STAGES = 4
TIME_STEP = 0.8
SHIP_SPEED = 0.5
EPSILON = 1e-06
MESH = pl.DeviceIdType.MESH
SUB = 8
LANE = 128
NSUM = 10
FOLD = 5
WIDE = 13
EXTRA = [10, 7, 4, 0]

THETA = [(m + 0.5) * math.pi / LEVELS for m in range(LEVELS)]
LAM = [2.0 * math.cos(t) - 2.0 for t in THETA]
WEIGHT = [(-1.0) ** m / math.tan(t / 2) / LEVELS for m, t in enumerate(THETA)]
TOPROW = [
    (math.cos((LEVELS - 2) * t) - 4.0 * math.cos((LEVELS - 1) * t)) * w
    for t, w in zip(THETA, WEIGHT)
]


def masks(shape):
    lane = lax.broadcasted_iota(jnp.int32, shape, len(shape) - 1)
    sub = lax.broadcasted_iota(jnp.int32, shape, len(shape) - 2)
    first = lane == 0
    last = lane == LANE - 1
    return first, first & (sub == 0), last, last & (sub == SUB - 1)


def before(v, mask):
    first, start, _, _ = mask
    r = pltpu.roll(v, 1, axis=2)
    return jnp.where(start, 0.0, jnp.where(first, pltpu.roll(r, 1, axis=1), r))


def after(v, mask):
    _, _, last, end = mask
    r = pltpu.roll(v, LANE - 1, axis=2)
    return jnp.where(end, 0.0, jnp.where(last, pltpu.roll(r, SUB - 1, axis=1), r))


def neighbours(v):
    mid = v[1:-1]
    mask = masks(mid.shape)
    return (v[2:] + v[:-2]) + (before(mid, mask) + after(mid, mask))


def step_sizes(g):
    g00, g01, g02, g03, g11, g12, g13, g22, g23, g33 = g
    gram = [[g00, g01, g02, g03], [g01, g11, g12, g13], [g02, g12, g22, g23], [g03, g13, g23, g33]]

    def quad(c, left, right):
        total = None
        for i, ci in enumerate(c):
            for j, cj in enumerate(c):
                if left == right and j < i:
                    continue
                term = ci * cj * gram[i + left][j + right]
                if left == right and j > i:
                    term = 2.0 * term
                total = term if total is None else total + term
        return total

    coef = [jnp.ones_like(g00)]
    beta = [0.0, 0.0, 0.0]
    for sweep in range(3):
        rr = quad(coef, 0, 0)
        re = quad(coef, 0, 1)
        ee = quad(coef, 1, 1)
        inv = 1.0 / (jnp.maximum(rr + 2.0 * re + ee, 0.0) + EPSILON)
        s = (rr + re) * inv
        t = (re + ee + EPSILON) * inv
        for j, c in enumerate(coef):
            beta[j] = beta[j] + s * c
        nxt = [t * c for c in coef] + [jnp.zeros_like(s)]
        for j, c in enumerate(coef):
            nxt[j + 1] = nxt[j + 1] - s * c
        coef = nxt
    return beta


def kernel(
    tiles, slices, rows, state_ref, depth_ref, press_ref, out_ref,
    raw, raw_d, raw_p, x, dm, wfac, coarse, first, total, planes, edge, part, slots, chain, chain_in,
    load_s, halo_s, halo_r, sum_s, sum_r, chain_s, chain_r,
):
    me = lax.axis_index("tile")
    cut = lax.axis_index("cuts")
    has_lo = me > 0
    has_hi = me < tiles - 1
    has_prev = cut > 0
    has_next = cut < slices - 1
    chunks = [(a, min(4, rows - a)) for a in range(0, rows, 4)]
    end = WIDE + rows

    loads = [
        pltpu.make_async_copy(state_ref.at[0], raw, load_s.at[0]),
        pltpu.make_async_copy(depth_ref, raw_d, load_s.at[1]),
        pltpu.make_async_copy(press_ref, raw_p, load_s.at[2]),
    ]
    for load in loads:
        load.start()

    x[:, 0:WIDE] = jnp.zeros((4, WIDE, SUB, LANE), jnp.float32)
    x[:, end : end + WIDE] = jnp.zeros((4, WIDE, SUB, LANE), jnp.float32)

    barrier = pltpu.get_barrier_semaphore()
    for d in range(1, tiles):
        pl.semaphore_signal(
            barrier, inc=1, device_id={"tile": lax.rem(me + d, tiles)}, device_id_type=MESH
        )

    @pl.when(has_prev)
    def _():
        pl.semaphore_signal(barrier, inc=1, device_id={"cuts": cut - 1}, device_id_type=MESH)

    @pl.when(has_next)
    def _():
        pl.semaphore_signal(barrier, inc=1, device_id={"cuts": cut + 1}, device_id_type=MESH)

    for load in loads:
        load.wait()
    for j in range(SUB):
        cols = slice(j * LANE, (j + 1) * LANE)
        x[0, WIDE:end, j, :] = raw[1, :, cols]
        x[1, WIDE:end, j, :] = raw_d[:, cols]
        x[2, WIDE:end, j, :] = raw[0, :, cols]
        x[3, WIDE:end, j, :] = raw_p[:, cols]

    parts = [(0, 2, 0, 4), (0, 2, 4, WIDE - 4), (2, 2, 0, WIDE - 2)]

    def halo_copy(k, side):
        p, np_, a, size = parts[k]
        if side == 0:
            src, dst = WIDE + a, end + a
        else:
            src, dst = end - a - size, WIDE - a - size
        return pltpu.make_async_remote_copy(
            src_ref=x.at[pl.ds(p, np_), pl.ds(src, size)],
            dst_ref=x.at[pl.ds(p, np_), pl.ds(dst, size)],
            send_sem=halo_s.at[k, side],
            recv_sem=halo_r.at[k, side],
            device_id={"tile": me - 1 if side == 0 else me + 1},
            device_id_type=MESH,
        )

    def halo_both(k, act):
        @pl.when(has_lo)
        def _():
            act(k, 0)

        @pl.when(has_hi)
        def _():
            act(k, 1)

    start = lambda k, side: halo_copy(k, side).start()
    arrive = lambda k, side: halo_copy(k, 1 - side).wait_recv()
    leave = lambda k, side: halo_copy(k, side).wait_send()

    def columns(a, b, inside):
        safe = x[1, a:b]
        if inside is not None:
            safe = jnp.where(inside, safe, 1.0)
        vert = LEVELS / safe
        vert = vert * vert
        for m in range(LEVELS):
            inverse = 1.0 / (vert * LAM[m] - 4.0)
            dm[m, a:b] = inverse if inside is None else jnp.where(inside, inverse, 0.0)
        wfac[a:b] = (0.5 * LEVELS) / safe

    columns(WIDE, end, None)
    own = x[1, WIDE:end]
    stiff = jnp.tanh(own)
    z = TIME_STEP * TIME_STEP * stiff
    cosine = 1.0 + z * (-1 / 2 + z * (1 / 24 + z * (-1 / 720 + z * (1 / 40320 - z / 3628800))))
    sine = TIME_STEP * (
        1.0 + z * (-1 / 6 + z * (1 / 120 + z * (-1 / 5040 + z * (1 / 362880 - z / 39916800))))
    )
    coarse[0] = cosine
    coarse[1] = stiff * sine
    coarse[2] = -sine

    pl.semaphore_wait(
        barrier, tiles - 1 + has_prev.astype(jnp.int32) + has_next.astype(jnp.int32)
    )
    for k in range(3):
        halo_both(k, start)

    halo_both(0, arrive)
    columns(WIDE - 3, WIDE, has_lo)
    columns(end, end + 3, has_hi)

    def sum_copy(s, d):
        return pltpu.make_async_remote_copy(
            src_ref=part.at[s],
            dst_ref=slots.at[s, d],
            send_sem=sum_s.at[s, d],
            recv_sem=sum_r.at[s, d],
            device_id={"tile": lax.rem(me + d, tiles)},
            device_id_type=MESH,
        )

    half = lax.broadcasted_iota(jnp.int32, (1, LANE), 1) < LANE // 2

    def inner_products(s):
        top = x[0, WIDE - 4 : end + 4]
        r0 = 4.0 * top[1:-1] - neighbours(top)
        u0 = r0[3:-3]
        gram = [None] * 9
        for m in range(LEVELS):
            c0 = dm[m, WIDE - 3 : end + 3] * r0
            u1 = neighbours(c0)
            c1 = dm[m, WIDE - 2 : end + 2] * u1
            u2 = neighbours(c1)
            c2 = dm[m, WIDE - 1 : end + 1] * u2
            u3 = neighbours(c2)
            us = [u0, u1[2:-2], u2[1:-1], u3]
            cs = [c0[3:-3], c1[2:-2], c2[1:-1]]
            k = 0
            for i in range(4):
                for j in range(max(i, 1), 4):
                    p = (4.0 * WEIGHT[m] ** 2) * jnp.sum(us[i] * us[j], axis=0)
                    gram[k] = p if gram[k] is None else gram[k] + p
                    k += 1
            for i in range(3):
                a = WEIGHT[m] * us[i + 1]
                b = TOPROW[m] * cs[i]
                if m == 0:
                    planes[i] = a
                    planes[3 + i] = b
                else:
                    planes[i] += a
                    planes[3 + i] += b
        bottom = [u0, planes[0], planes[1], planes[2]]
        k = 0
        for i in range(4):
            for j in range(max(i, 1), 4):
                gram[k] = gram[k] + 0.5 * jnp.sum(bottom[i] * bottom[j], axis=0)
                k += 1
        gram = [LEVELS * jnp.sum(u0 * u0, axis=0)] + gram
        gram = [jnp.sum(g, axis=0, keepdims=True) for g in gram]
        for k in range(FOLD):
            a, b = gram[k], gram[k + FOLD]
            part[s, k : k + 1] = jnp.where(half, a, b) + pltpu.roll(
                jnp.where(half, b, a), LANE // 2, axis=1
            )

    def beyond(side, a, b):
        top = x[0, a - 3 : b + 3]
        r0 = 4.0 * top[1:-1] - neighbours(top)
        size = b - a
        for m in range(LEVELS):
            c0 = dm[m, a - 2 : b + 2] * r0
            c1 = dm[m, a - 1 : b + 1] * neighbours(c0)
            c2 = dm[m, a:b] * neighbours(c1)
            for i, c in enumerate([c0[2:-2], c1[1:-1], c2]):
                v = TOPROW[m] * c
                if m == 0:
                    edge[side, i, 0:size] = v
                else:
                    edge[side, i, 0:size] += v

    def explicit(a, b):
        elev = x[2, a:b]
        phi = x[0, a:b]
        mask = masks(elev.shape)
        he = 0.5 * (x[2, a + 1 : b + 1] - x[2, a - 1 : b - 1])
        fe = 0.5 * (x[0, a + 1 : b + 1] - x[0, a - 1 : b - 1])
        hn = 0.5 * (after(elev, mask) - before(elev, mask))
        fn = 0.5 * (after(phi, mask) - before(phi, mask))
        slope = 1.0 + he * he + hn * hn
        rate_h = SHIP_SPEED * he - (he * fe + hn * fn)
        rate_f = SHIP_SPEED * fe - elev - 0.5 * (fe * fe + fn * fn) - x[3, a:b]
        return slope, rate_h, rate_f

    for s in range(STAGES):
        extra = EXTRA[s]
        inner_products(s)
        for d in range(1, tiles):
            sum_copy(s, d).start()

        if s == 0:
            halo_both(1, arrive)
            halo_both(2, arrive)
            columns(1, WIDE - 3, has_lo)
            columns(end + 3, end + WIDE - 1, has_hi)
            first[0] = x[2]
            first[1] = x[0]
        regions = [(WIDE, end, None)]
        if extra:
            beyond(0, WIDE - extra, WIDE)
            beyond(1, end, end + extra)
            regions += [(WIDE - extra, WIDE, 0), (end, end + extra, 1)]
        known = [explicit(a, b) for a, b, _ in regions]
        if s == 0:
            for k in range(3):
                halo_both(k, leave)

        for d in range(1, tiles):
            sum_copy(s, d).wait_recv()
        whole = part[s]
        for d in range(1, tiles):
            whole = whole + slots[s, d]
        low = jnp.sum(jnp.where(half, whole, 0.0), axis=1, keepdims=True)
        high = jnp.sum(jnp.where(half, 0.0, whole), axis=1, keepdims=True)
        sums = [low[k : k + 1] for k in range(FOLD)] + [high[k : k + 1] for k in range(FOLD)]
        beta = [jnp.broadcast_to(b, (SUB, LANE)) for b in step_sizes(sums)]

        share = (1.0 if s in (0, STAGES - 1) else 2.0) * (TIME_STEP / 6.0)
        ahead = TIME_STEP if s == STAGES - 2 else 0.5 * TIME_STEP
        for (a, b, side), (slope, rate_h, rate_f) in zip(regions, known):
            if side is None:
                y = [planes[3 + i] for i in range(3)]
            else:
                y = [edge[side, i, 0 : b - a] for i in range(3)]
            w = (beta[0] * y[0] + beta[1] * y[1] + beta[2] * y[2]) * wfac[a:b]
            ws = w * slope
            rate_h = rate_h + ws
            rate_f = rate_f + 0.5 * w * ws
            if side is None:
                if s == 0:
                    total[0] = first[0, a:b] + share * rate_h
                    total[1] = first[1, a:b] + share * rate_f
                else:
                    total[0] += share * rate_h
                    total[1] += share * rate_f
            if s < STAGES - 1:
                new_h = first[0, a:b] + ahead * rate_h
                new_f = first[1, a:b] + ahead * rate_f
                if side is not None:
                    there = has_hi if side else has_lo
                    new_h = jnp.where(there, new_h, 0.0)
                    new_f = jnp.where(there, new_f, 0.0)
                x[2, a:b] = new_h
                x[0, a:b] = new_f

    def chain_copy(k):
        a, size = chunks[k]
        return pltpu.make_async_remote_copy(
            src_ref=chain.at[pl.ds(a, size)],
            dst_ref=chain_in.at[pl.ds(a, size)],
            send_sem=chain_s.at[k],
            recv_sem=chain_r.at[k],
            device_id={"cuts": cut + 1},
            device_id_type=MESH,
        )

    @pl.when(has_prev)
    def _():
        e = first[0, WIDE:end]
        p = first[1, WIDE:end]
        total[0] = total[0] - (coarse[0] * e + coarse[1] * p)
        total[1] = total[1] - (coarse[2] * e + coarse[0] * p)

    for k, (a, size) in enumerate(chunks):
        span = slice(a, a + size)

        @pl.when(has_prev)
        def _():
            chain_copy(k).wait_recv()
            e = chain_in[span, 0]
            p = chain_in[span, 1]
            chain[span, 0] = coarse[0, span] * e + coarse[1, span] * p + total[0, span]
            chain[span, 1] = coarse[2, span] * e + coarse[0, span] * p + total[1, span]

        @pl.when(jnp.logical_not(has_prev))
        def _():
            chain[span, 0] = total[0, span]
            chain[span, 1] = total[1, span]

        @pl.when(has_next)
        def _():
            chain_copy(k).start()

    for j in range(SUB):
        cols = slice(j * LANE, (j + 1) * LANE)
        for c in range(2):
            out_ref[0, c, :, cols] = chain[:, c, j, :]

    @pl.when(has_next)
    def _():
        for k in range(len(chunks)):
            chain_copy(k).wait_send()

    for s in range(STAGES):
        for d in range(1, tiles):
            sum_copy(s, d).wait_send()


def local(tiles, slices, state_in, sea_depth, pressure):
    rows = sea_depth.shape[0]
    plane = (rows, SUB, LANE)
    wide = rows + 2 * WIDE
    f32 = jnp.float32
    chunks = -(-rows // 4)
    return pl.pallas_call(
        functools.partial(kernel, tiles, slices, rows),
        out_shape=jax.ShapeDtypeStruct(state_in.shape, f32),
        in_specs=[pl.BlockSpec(memory_space=pltpu.HBM)] * 3,
        out_specs=pl.BlockSpec(memory_space=pltpu.VMEM),
        scratch_shapes=[
            pltpu.VMEM(state_in.shape[1:], f32),
            pltpu.VMEM(sea_depth.shape, f32),
            pltpu.VMEM(pressure.shape, f32),
            pltpu.VMEM((4, wide, SUB, LANE), f32),
            pltpu.VMEM((LEVELS, wide, SUB, LANE), f32),
            pltpu.VMEM((wide, SUB, LANE), f32),
            pltpu.VMEM((3,) + plane, f32),
            pltpu.VMEM((2, wide, SUB, LANE), f32),
            pltpu.VMEM((2,) + plane, f32),
            pltpu.VMEM((6,) + plane, f32),
            pltpu.VMEM((2, 3, EXTRA[0], SUB, LANE), f32),
            pltpu.VMEM((STAGES, FOLD, LANE), f32),
            pltpu.VMEM((STAGES, tiles, FOLD, LANE), f32),
            pltpu.VMEM((rows, 2, SUB, LANE), f32),
            pltpu.VMEM((rows, 2, SUB, LANE), f32),
            pltpu.SemaphoreType.DMA((3,)),
            pltpu.SemaphoreType.DMA((3, 2)),
            pltpu.SemaphoreType.DMA((3, 2)),
            pltpu.SemaphoreType.DMA((STAGES, tiles)),
            pltpu.SemaphoreType.DMA((STAGES, tiles)),
            pltpu.SemaphoreType.DMA((chunks,)),
            pltpu.SemaphoreType.DMA((chunks,)),
        ],
        compiler_params=pltpu.CompilerParams(
            collective_id=0, has_side_effects=True, vmem_limit_bytes=48 * 1024 * 1024
        ),
        name="wake_step",
    )(state_in, sea_depth, pressure)


def solution(mesh):
    placed = (P("cuts", None, "tile", None), P("tile", None), P("tile", None))
    return jax.shard_map(
        functools.partial(local, mesh.shape["tile"], mesh.shape["cuts"]),
        mesh=mesh,
        in_specs=placed,
        out_specs=P("cuts", None, "tile", None),
        check_vma=False,
    )
```

profile of v0, /device:TPU:3, one launch (start us, length us, event | category | flops | bytes accessed | tf_op | source)
XLA Modules:
  0.0 44.6 jit_solution(4129686915582529605)
XLA Ops:
  0.0 0.0 copy-start
  0.0 0.9 %copy-done = f32[1,2,16,1024]{3,2,1,0:T(8,128)S(1)} copy-done((f32[1,2,16,1024]{3,2,1,0:T(8,128)S(1)}, f32[1,2,16,1024]{3,2,1,0:T(8,128)}, u32[]{:S(2)}) %copy-start) | copy-done | bytes 131096
  0.9 0.0 copy-start.1
  0.9 0.8 %copy-done.1 = f32[16,1024]{1,0:T(8,128)S(1)} copy-done((f32[16,1024]{1,0:T(8,128)S(1)}, f32[16,1024]{1,0:T(8,128)}, u32[]{:S(2)}) %copy-start.1) | copy-done | bytes 65560
  1.7 0.0 copy-start.2
  1.7 0.8 %copy-done.2 = f32[16,1024]{1,0:T(8,128)S(1)} copy-done((f32[16,1024]{1,0:T(8,128)S(1)}, f32[16,1024]{1,0:T(8,128)}, u32[]{:S(2)}) %copy-start.2) | copy-done | bytes 65560
  2.6 41.4 %wake_step.1 = f32[1,2,16,1024]{3,2,1,0:T(8,128)S(1)} custom-call(f32[1,2,16,1024]{3,2,1,0:T(8,128)S(1)} %copy-done, f32[16,1024]{1,0:T(8,128)S(1)} %copy-done.1, f32[16,1024]{1,0:T(8,128)S(1)} %copy-done.2), custom_call_target="tpu_custom_call" | custom-call | tf_op jit(solution)/shard_map/wake_step/pallas_call | solution.py:407
  44.0 0.7 %copy.5 = f32[1,2,16,1024]{3,2,1,0:T(8,128)} copy(f32[1,2,16,1024]{3,2,1,0:T(8,128)S(1)} %wake_step.1) | data formatting | bytes 262144
Async XLA Ops:
  0.0 0.9 %copy-start = (f32[1,2,16,1024]{3,2,1,0:T(8,128)S(1)}, f32[1,2,16,1024]{3,2,1,0:T(8,128)}, u32[]{:S(2)}) copy-start(f32[1,2,16,1024]{3,2,1,0:T(8,128)} %state_ref.1) | copy-start | bytes 393220
  0.9 0.8 %copy-start.1 = (f32[16,1024]{1,0:T(8,128)S(1)}, f32[16,1024]{1,0:T(8,128)}, u32[]{:S(2)}) copy-start(f32[16,1024]{1,0:T(8,128)} %depth_ref.1) | copy-start | bytes 196612
  1.7 0.8 %copy-start.2 = (f32[16,1024]{1,0:T(8,128)S(1)}, f32[16,1024]{1,0:T(8,128)}, u32[]{:S(2)}) copy-start(f32[16,1024]{1,0:T(8,128)} %press_ref.1) | copy-start | bytes 196612
where the time goes:
time: 44.8 us; the launch traced here: 44.6 us
  Pallas kernels  41.4 us (92%)
  local copies, waits for them, and re-layouts  3.24 us (7%)
    pallas_call x1, Pallas kernels, local(): pl.pallas_call(functools.partial(kernel, tiles, slices, rows), out_shape=...  41.4 us
    unnamed x7, local copies, waits for them, and re-layouts  3.24 us

commit v1 on v0

--- a/solution.py
+++ b/solution.py
@@ -434,7 +434,7 @@
             pltpu.SemaphoreType.DMA((chunks,)),
         ],
         compiler_params=pltpu.CompilerParams(
-            collective_id=0, has_side_effects=True, vmem_limit_bytes=48 * 1024 * 1024
+            collective_id=0, has_side_effects=True, vmem_limit_bytes=60 * 1024 * 1024
         ),
         name="wake_step",
     )(state_in, sea_depth, pressure)

time: 44.8 us -> 43.4 us (0.969)
  local copies, waits for them, and re-layouts: 3.24 us -> 1.57 us
    unnamed x7 -> x1, local copies, waits for them, and re-layouts: 3.24 us -> 1.57 us
where the time goes in v1:
time: 43.4 us; the launch traced here: 43.3 us
  Pallas kernels  41.7 us (96%)
  local copies, waits for them, and re-layouts  1.57 us (4%)
    pallas_call x1, Pallas kernels, local(): pl.pallas_call(functools.partial(kernel, tiles, slices, rows), out_shape=...  41.7 us
    unnamed x1, local copies, waits for them, and re-layouts  1.57 us

profile of v1, /device:TPU:3, one launch (start us, length us, event | category | flops | bytes accessed | tf_op | source)
XLA Modules:
  0.0 43.3 jit_solution(7371425455476697366)
XLA Ops:
  0.0 41.7 %wake_step.1 = f32[1,2,16,1024]{3,2,1,0:T(8,128)} custom-call(f32[1,2,16,1024]{3,2,1,0:T(8,128)} %state_ref.1, f32[16,1024]{1,0:T(8,128)} %depth_ref.1, f32[16,1024]{1,0:T(8,128)} %press_ref.1), custom_call_target="tpu_custom_call" | custom-call | tf_op jit(solution)/shard_map/wake_step/pallas_call | solution.py:407
  41.7 1.6 %copy.5 = f32[1,2,16,1024]{3,2,1,0:T(8,128)} copy(f32[1,2,16,1024]{3,2,1,0:T(8,128)} %wake_step.1) | data formatting | bytes 262144

commit v2 on v1

v2 whole, which is shorter than its diff:
```python
import functools
import math

import jax
import jax.numpy as jnp
from jax import lax
from jax.experimental import pallas as pl
from jax.experimental.pallas import tpu as pltpu
from jax.sharding import PartitionSpec as P

LEVELS = 8
STAGES = 4
TIME_STEP = 0.8
SHIP_SPEED = 0.5
EPSILON = 1e-06
MESH = pl.DeviceIdType.MESH
SUB = 8
LANE = 128
FOLD = 5
PAD = 16
SPAN = 24
PARTS = [(0, 2, 0, 4), (0, 2, 4, 3), (2, 2, 0, 5), (0, 2, 7, 6), (2, 2, 5, 6)]
NEAR_PARTS = [1, 2]
FAR_PARTS = [3, 4]

THETA = [(m + 0.5) * math.pi / LEVELS for m in range(LEVELS)]
LAM = [2.0 * math.cos(t) - 2.0 for t in THETA]
WEIGHT = [(-1.0) ** m / math.tan(t / 2) / LEVELS for m, t in enumerate(THETA)]
TOPROW = [math.cos((LEVELS - 2) * t) - 4.0 * math.cos((LEVELS - 1) * t) for t in THETA]


def rolled(v):
    lane = lax.broadcasted_iota(jnp.int32, (1,) + v.shape[1:], 2)
    r = pltpu.roll(v, 1, axis=2)
    l = pltpu.roll(v, LANE - 1, axis=2)
    zero = jnp.zeros_like(v[:1])
    before = jnp.where(lane == 0, jnp.concatenate([zero, r[:-1]], axis=0), r)
    after = jnp.where(lane == LANE - 1, jnp.concatenate([l[1:], zero], axis=0), l)
    return before, after


def rows8(ref, a):
    return ref[:, a : a + SUB]


def neighbours(ref, a):
    before, after = rolled(rows8(ref, a))
    return (rows8(ref, a + 1) + rows8(ref, a - 1)) + (before + after)


def step_sizes(g):
    g00, g01, g02, g03, g11, g12, g13, g22, g23, g33 = g
    gram = [[g00, g01, g02, g03], [g01, g11, g12, g13], [g02, g12, g22, g23], [g03, g13, g23, g33]]

    def quad(c, left, right):
        total = None
        for i, ci in enumerate(c):
            for j, cj in enumerate(c):
                if left == right and j < i:
                    continue
                term = ci * cj * gram[i + left][j + right]
                if left == right and j > i:
                    term = 2.0 * term
                total = term if total is None else total + term
        return total

    coef = [jnp.ones_like(g00)]
    beta = [0.0, 0.0, 0.0]
    for sweep in range(3):
        rr = quad(coef, 0, 0)
        re = quad(coef, 0, 1)
        ee = quad(coef, 1, 1)
        inv = 1.0 / (jnp.maximum(rr + 2.0 * re + ee, 0.0) + EPSILON)
        s = (rr + re) * inv
        t = (re + ee + EPSILON) * inv
        for j, c in enumerate(coef):
            beta[j] = beta[j] + s * c
        nxt = [t * c for c in coef] + [jnp.zeros_like(s)]
        for j, c in enumerate(coef):
            nxt[j + 1] = nxt[j + 1] - s * c
        coef = nxt
    return beta


def kernel(
    tiles, slices, rows, state_ref, depth_ref, press_ref, out_ref,
    raw, raw_d, raw_p, x, later, dm, dw, wfac, coarse, total, res, c, u, planes, top, out_c, out_y,
    part, slots, chain, chain_in,
    load_s, halo_s, halo_r, sum_s, sum_r, chain_s, chain_r,
):
    me = lax.axis_index("tile")
    cut = lax.axis_index("cuts")
    has_lo = me > 0
    has_hi = me < tiles - 1
    has_prev = cut > 0
    has_next = cut < slices - 1
    blocks = x.shape[1]
    end = PAD + rows
    own = list(range(PAD, end, SUB))
    wide = list(range(PAD - 3, end - 5, SUB)) + [end - 5]
    wide = sorted(set(wide))

    loads = [
        pltpu.make_async_copy(state_ref.at[0], raw, load_s.at[0]),
        pltpu.make_async_copy(depth_ref, raw_d, load_s.at[1]),
        pltpu.make_async_copy(press_ref, raw_p, load_s.at[2]),
    ]
    for load in loads:
        load.start()

    for p in range(4):
        x[p, :, 0:PAD] = jnp.zeros((blocks, PAD, LANE), jnp.float32)
        x[p, :, end : end + PAD] = jnp.zeros((blocks, PAD, LANE), jnp.float32)

    barrier = pltpu.get_barrier_semaphore()
    for d in range(1, tiles):
        pl.semaphore_signal(
            barrier, inc=1, device_id={"tile": lax.rem(me + d, tiles)}, device_id_type=MESH
        )

    @pl.when(has_prev)
    def _():
        pl.semaphore_signal(barrier, inc=1, device_id={"cuts": cut - 1}, device_id_type=MESH)

    @pl.when(has_next)
    def _():
        pl.semaphore_signal(barrier, inc=1, device_id={"cuts": cut + 1}, device_id_type=MESH)

    for load in loads:
        load.wait()
    for j in range(blocks):
        cols = slice(j * LANE, (j + 1) * LANE)
        x[0, j, PAD:end] = raw[1, :, cols]
        x[1, j, PAD:end] = raw_d[:, cols]
        x[2, j, PAD:end] = raw[0, :, cols]
        x[3, j, PAD:end] = raw_p[:, cols]

    def halo_copy(k, side):
        p, count, a, size = PARTS[k]
        if side == 0:
            src, dst = PAD + a, end + a
        else:
            src, dst = end - a - size, PAD - a - size
        return pltpu.make_async_remote_copy(
            src_ref=x.at[pl.ds(p, count), :, pl.ds(src, size)],
            dst_ref=x.at[pl.ds(p, count), :, pl.ds(dst, size)],
            send_sem=halo_s.at[k, side],
            recv_sem=halo_r.at[k, side],
            device_id={"tile": me - 1 if side == 0 else me + 1},
            device_id_type=MESH,
        )

    def halo_both(ks, act):
        @pl.when(has_lo)
        def _():
            for k in ks:
                act(k, 0)

        @pl.when(has_hi)
        def _():
            for k in ks:
                act(k, 1)

    start = lambda k, side: halo_copy(k, side).start()
    arrive = lambda k, side: halo_copy(k, 1 - side).wait_recv()
    leave = lambda k, side: halo_copy(k, side).wait_send()

    def columns(a, inside=None):
        safe = rows8(x.at[1], a)
        if inside is not None:
            safe = jnp.where(inside, safe, 1.0)
        inv_depth = 1.0 / safe
        vert = LEVELS * inv_depth
        vert = vert * vert
        for m in range(LEVELS):
            inverse = 1.0 / (vert * LAM[m] - 4.0)
            if inside is not None:
                inverse = jnp.where(inside, inverse, 0.0)
            dm[m, :, a : a + SUB] = inverse
            dw[m, :, a : a + SUB] = WEIGHT[m] * inverse
        wfac[:, a : a + SUB] = (0.5 * LEVELS) * inv_depth

    sub = lax.broadcasted_iota(jnp.int32, (1, SUB, LANE), 1)

    def edge_columns(a_lo, own_lo, a_hi, own_hi):
        columns(a_lo, sub + SUB * has_lo.astype(jnp.int32) >= own_lo)
        columns(a_hi, sub - SUB * has_hi.astype(jnp.int32) < own_hi)

    for a in own:
        columns(a)

    pl.semaphore_wait(
        barrier, tiles - 1 + has_prev.astype(jnp.int32) + has_next.astype(jnp.int32)
    )
    halo_both([0], start)
    halo_both(NEAR_PARTS, start)

    depth = x[1, :, PAD:end]
    stiff = jnp.tanh(depth)
    z = TIME_STEP * TIME_STEP * stiff
    coarse[0] = 1.0 + z * (-1 / 2 + z * (1 / 24 + z * (-1 / 720 + z * (1 / 40320 - z / 3628800))))
    sine = TIME_STEP * (
        1.0 + z * (-1 / 6 + z * (1 / 120 + z * (-1 / 5040 + z * (1 / 362880 - z / 39916800))))
    )
    coarse[1] = stiff * sine
    coarse[2] = -sine

    halo_both([0], arrive)
    edge_columns(PAD - 4, 4, end - 4, 4)

    def sum_copy(s, d):
        return pltpu.make_async_remote_copy(
            src_ref=part.at[s],
            dst_ref=slots.at[s, d],
            send_sem=sum_s.at[s, d],
            recv_sem=sum_r.at[s, d],
            device_id={"tile": lax.rem(me + d, tiles)},
            device_id_type=MESH,
        )

    half = lax.broadcasted_iota(jnp.int32, (1, LANE), 1) < LANE // 2

    def phi_of(s):
        return x.at[0] if s == 0 else later.at[s - 1, 0]

    def elev_of(s):
        return x.at[2] if s == 0 else later.at[s - 1, 1]

    def inner_products(s):
        phi = phi_of(s)
        for a in wide:
            res[:, a : a + SUB] = 4.0 * rows8(phi, a) - neighbours(phi, a)
        gram = [None] * 9

        def add(k, v):
            gram[k] = v if gram[k] is None else gram[k] + v

        for a in wide:
            r = rows8(res, a)
            for m in range(LEVELS):
                c[m, 0, :, a : a + SUB] = rows8(dw.at[m], a) * r
        for i in range(2):
            for m in range(LEVELS):
                for a in wide:
                    v = neighbours(c.at[m, i], a)
                    u[m, i, :, a : a + SUB] = v
                    c[m, i + 1, :, a : a + SUB] = rows8(dm.at[m], a) * v
        for m in range(LEVELS):
            for a in own:
                us = [rows8(res, a), rows8(u.at[m, 0], a), rows8(u.at[m, 1], a), neighbours(c.at[m, 2], a)]
                k = 0
                for i in range(4):
                    for j in range(max(i, 1), 4):
                        v = jnp.sum(us[i] * us[j], axis=0)
                        add(k, WEIGHT[m] * v if i == 0 else v)
                        k += 1
                for i in range(3):
                    if m == 0:
                        planes[i, :, a : a + SUB] = us[i + 1]
                    else:
                        planes[i, :, a : a + SUB] += us[i + 1]
        gram = [4.0 * g for g in gram]
        square = None
        for a in own:
            bottom = [rows8(res, a)] + [rows8(planes.at[i], a) for i in range(3)]
            k = 0
            for i in range(4):
                for j in range(max(i, 1), 4):
                    gram[k] = gram[k] + 0.5 * jnp.sum(bottom[i] * bottom[j], axis=0)
                    k += 1
            v = jnp.sum(bottom[0] * bottom[0], axis=0)
            square = v if square is None else square + v
        gram = [jnp.sum(g, axis=0, keepdims=True) for g in [LEVELS * square] + gram]
        for k in range(FOLD):
            a, b = gram[k], gram[k + FOLD]
            part[s, k : k + 1] = jnp.where(half, a, b) + pltpu.roll(
                jnp.where(half, b, a), LANE // 2, axis=1
            )

    def own_tops():
        for a in own:
            for i in range(3):
                y = None
                for m in range(LEVELS):
                    v = TOPROW[m] * rows8(c.at[m, i], a)
                    y = v if y is None else y + v
                top[i, :, a : a + SUB] = y

    def beyond(s, regions):
        phi = phi_of(s)
        for side, (_, first_rows, second_row, _) in enumerate(regions):
            base = second_row - SUB
            for a in first_rows:
                r = 4.0 * rows8(phi, a) - neighbours(phi, a)
                for m in range(LEVELS):
                    out_c[m, side, 0, :, a - base : a - base + SUB] = rows8(dw.at[m], a) * r
        for m in range(LEVELS):
            for side, (_, _, second_row, _) in enumerate(regions):
                out_c[m, side, 1, :, SUB : 2 * SUB] = rows8(dm.at[m], second_row) * neighbours(
                    out_c.at[m, side, 0], SUB
                )
        for side, (_, _, second_row, third_row) in enumerate(regions):
            at = third_row - second_row + SUB
            ys = [None] * 3
            for m in range(LEVELS):
                c0, c1 = out_c.at[m, side, 0], out_c.at[m, side, 1]
                c2 = rows8(dm.at[m], third_row) * neighbours(c1, at)
                for i, v in enumerate([rows8(c0, at), rows8(c1, at), c2]):
                    v = TOPROW[m] * v
                    ys[i] = v if ys[i] is None else ys[i] + v
            for i in range(3):
                out_y[side, i] = ys[i]

    def explicit(s, a):
        elev, phi = elev_of(s), phi_of(s)
        before_h, after_h = rolled(rows8(elev, a))
        before_f, after_f = rolled(rows8(phi, a))
        he = 0.5 * (rows8(elev, a + 1) - rows8(elev, a - 1))
        fe = 0.5 * (rows8(phi, a + 1) - rows8(phi, a - 1))
        hn = 0.5 * (after_h - before_h)
        fn = 0.5 * (after_f - before_f)
        slope = 1.0 + he * he + hn * hn
        rate_h = SHIP_SPEED * he - (he * fe + hn * fn)
        rate_f = SHIP_SPEED * fe - rows8(elev, a) - 0.5 * (fe * fe + fn * fn) - rows8(x.at[3], a)
        return slope, rate_h, rate_f

    def rates(beta, y, known, a):
        slope, rate_h, rate_f = known
        w = (beta[0] * y[0] + beta[1] * y[1] + beta[2] * y[2]) * rows8(wfac, a)
        ws = w * slope
        return rate_h + ws, rate_f + 0.5 * w * ws

    def advance(s, a, rate_h, rate_f, there=None):
        ahead = TIME_STEP if s == STAGES - 2 else 0.5 * TIME_STEP
        new_f = rows8(x.at[0], a) + ahead * rate_f
        new_h = rows8(x.at[2], a) + ahead * rate_h
        if there is not None:
            new_f = jnp.where(there, new_f, 0.0)
            new_h = jnp.where(there, new_h, 0.0)
        later[s, 0, :, a : a + SUB] = new_f
        later[s, 1, :, a : a + SUB] = new_h

    near = [
        (has_lo, [PAD - 6], PAD - 6, PAD - 4),
        (has_hi, [end - 2], end - 2, end - 4),
    ]
    far = {
        0: [
            (has_lo, [PAD - 12, PAD - 10], PAD - 11, PAD - 12),
            (has_hi, [end + 2, end + 4], end + 3, end + 4),
        ],
        1: [
            (has_lo, [PAD - 10], PAD - 10, PAD - 12),
            (has_hi, [end + 2], end + 2, end + 4),
        ],
    }
    betas = []

    for s in range(STAGES):
        inner_products(s)
        for d in range(1, tiles):
            sum_copy(s, d).start()
        own_tops()
        known = [explicit(s, a) for a in own] if s > 0 else None
        if s == 0:
            halo_both(FAR_PARTS, start)
            halo_both(NEAR_PARTS, arrive)
            edge_columns(PAD - 7, 7, end - 1, 1)
            known = [explicit(s, a) for a in own]
        if s == 1:
            halo_both(FAR_PARTS, arrive)
            edge_columns(PAD - 13, SUB, end + 5, 0)
        if s - 1 in far:
            beyond(s - 1, far[s - 1])
            for side, (there, _, _, third_row) in enumerate(far[s - 1]):
                y = [out_y[side, i] for i in range(3)]
                seen = explicit(s - 1, third_row)
                rate_h, rate_f = rates(betas[s - 1], y, seen, third_row)
                advance(s - 1, third_row, rate_h, rate_f, there)
        if s < STAGES - 1:
            beyond(s, near)
            known_near = [explicit(s, third_row) for _, _, _, third_row in near]

        for d in range(1, tiles):
            sum_copy(s, d).wait_recv()
        whole = part[s]
        for d in range(1, tiles):
            whole = whole + slots[s, d]
        low = jnp.sum(jnp.where(half, whole, 0.0), axis=1, keepdims=True)
        high = jnp.sum(jnp.where(half, 0.0, whole), axis=1, keepdims=True)
        sums = [low[k : k + 1] for k in range(FOLD)] + [high[k : k + 1] for k in range(FOLD)]
        betas.append([jnp.broadcast_to(b, (SUB, LANE)) for b in step_sizes(sums)])

        if s < STAGES - 1:
            for side, (there, _, _, third_row) in enumerate(near):
                y = [out_y[side, i] for i in range(3)]
                rate_h, rate_f = rates(betas[s], y, known_near[side], third_row)
                advance(s, third_row, rate_h, rate_f, there)
        share = (1.0 if s in (0, STAGES - 1) else 2.0) * (TIME_STEP / 6.0)
        for a, seen in zip(own, known):
            y = [rows8(top.at[i], a) for i in range(3)]
            rate_h, rate_f = rates(betas[s], y, seen, a)
            if s < STAGES - 1:
                advance(s, a, rate_h, rate_f)
            b = a - PAD
            if s == 0:
                total[0, :, b : b + SUB] = rows8(x.at[2], a) + share * rate_h
                total[1, :, b : b + SUB] = rows8(x.at[0], a) + share * rate_f
            else:
                total[0, :, b : b + SUB] += share * rate_h
                total[1, :, b : b + SUB] += share * rate_f

    chunk = 2
    pieces = list(range(0, blocks, chunk))

    def chain_copy(k):
        return pltpu.make_async_remote_copy(
            src_ref=chain.at[pl.ds(pieces[k], chunk)],
            dst_ref=chain_in.at[pl.ds(pieces[k], chunk)],
            send_sem=chain_s.at[k],
            recv_sem=chain_r.at[k],
            device_id={"cuts": cut + 1},
            device_id_type=MESH,
        )

    @pl.when(has_prev)
    def _():
        e = x[2, :, PAD:end]
        p = x[0, :, PAD:end]
        total[0] = total[0] - (coarse[0] * e + coarse[1] * p)
        total[1] = total[1] - (coarse[2] * e + coarse[0] * p)

    for k, first in enumerate(pieces):
        span = slice(first, first + chunk)

        @pl.when(has_prev)
        def _():
            chain_copy(k).wait_recv()
            e = chain_in[span, 0]
            p = chain_in[span, 1]
            chain[span, 0] = coarse[0, span] * e + coarse[1, span] * p + total[0, span]
            chain[span, 1] = coarse[2, span] * e + coarse[0, span] * p + total[1, span]

        @pl.when(jnp.logical_not(has_prev))
        def _():
            chain[span, 0] = total[0, span]
            chain[span, 1] = total[1, span]

        @pl.when(has_next)
        def _():
            chain_copy(k).start()

    for j in range(blocks):
        for k in range(2):
            out_ref[0, k, :, j * LANE : (j + 1) * LANE] = chain[j, k]

    halo_both(range(len(PARTS)), leave)

    @pl.when(has_next)
    def _():
        for k in range(len(pieces)):
            chain_copy(k).wait_send()

    for s in range(STAGES):
        for d in range(1, tiles):
            sum_copy(s, d).wait_send()


def local(tiles, slices, state_in, sea_depth, pressure):
    rows, columns = sea_depth.shape
    blocks = columns // LANE
    field = (blocks, rows + 2 * PAD, LANE)
    plane = (blocks, rows, LANE)
    f32 = jnp.float32
    pieces = blocks // 2
    return pl.pallas_call(
        functools.partial(kernel, tiles, slices, rows),
        out_shape=jax.ShapeDtypeStruct(state_in.shape, f32),
        in_specs=[pl.BlockSpec(memory_space=pltpu.HBM)] * 3,
        out_specs=pl.BlockSpec(memory_space=pltpu.VMEM),
        scratch_shapes=[
            pltpu.VMEM(state_in.shape[1:], f32),
            pltpu.VMEM(sea_depth.shape, f32),
            pltpu.VMEM(pressure.shape, f32),
            pltpu.VMEM((4,) + field, f32),
            pltpu.VMEM((STAGES - 1, 2) + field, f32),
            pltpu.VMEM((LEVELS,) + field, f32),
            pltpu.VMEM((LEVELS,) + field, f32),
            pltpu.VMEM(field, f32),
            pltpu.VMEM((3,) + plane, f32),
            pltpu.VMEM((2,) + plane, f32),
            pltpu.VMEM(field, f32),
            pltpu.VMEM((LEVELS, 3) + field, f32),
            pltpu.VMEM((LEVELS, 2) + field, f32),
            pltpu.VMEM((3,) + field, f32),
            pltpu.VMEM((3,) + field, f32),
            pltpu.VMEM((LEVELS, 2, 2, blocks, SPAN, LANE), f32),
            pltpu.VMEM((2, 3, blocks, SUB, LANE), f32),
            pltpu.VMEM((STAGES, FOLD, LANE), f32),
            pltpu.VMEM((STAGES, tiles, FOLD, LANE), f32),
            pltpu.VMEM((blocks, 2, rows, LANE), f32),
            pltpu.VMEM((blocks, 2, rows, LANE), f32),
            pltpu.SemaphoreType.DMA((3,)),
            pltpu.SemaphoreType.DMA((len(PARTS), 2)),
            pltpu.SemaphoreType.DMA((len(PARTS), 2)),
            pltpu.SemaphoreType.DMA((STAGES, tiles)),
            pltpu.SemaphoreType.DMA((STAGES, tiles)),
            pltpu.SemaphoreType.DMA((pieces,)),
            pltpu.SemaphoreType.DMA((pieces,)),
        ],
        compiler_params=pltpu.CompilerParams(
            collective_id=0, has_side_effects=True, vmem_limit_bytes=60 * 1024 * 1024
        ),
        name="wake_step",
    )(state_in, sea_depth, pressure)


def solution(mesh):
    placed = (P("cuts", None, "tile", None), P("tile", None), P("tile", None))
    return jax.shard_map(
        functools.partial(local, mesh.shape["tile"], mesh.shape["cuts"]),
        mesh=mesh,
        in_specs=placed,
        out_specs=P("cuts", None, "tile", None),
        check_vma=False,
    )
```

time: 43.4 us -> 40.1 us (0.924)
  Pallas kernels: 41.7 us -> 38.3 us
    pallas_call x1, Pallas kernels: 41.7 us -> 38.3 us  [local(): pl.pallas_call(functools.partial(kernel, tiles, slices, rows), out_shape=...]
where the time goes in v2:
time: 40.1 us; the launch traced here: 39.9 us
  Pallas kernels  38.3 us (96%)
  local copies, waits for them, and re-layouts  1.57 us (4%)
    pallas_call x1, Pallas kernels, local(): pl.pallas_call(functools.partial(kernel, tiles, slices, rows), out_shape=...  38.3 us
    unnamed x1, local copies, waits for them, and re-layouts  1.57 us

profile of v2, /device:TPU:3, one launch (start us, length us, event | category | flops | bytes accessed | tf_op | source)
XLA Modules:
  0.0 39.9 jit_solution(1860917697868381083)
XLA Ops:
  0.0 38.3 %wake_step.1 = f32[1,2,16,1024]{3,2,1,0:T(8,128)} custom-call(f32[1,2,16,1024]{3,2,1,0:T(8,128)} %state_ref.1, f32[16,1024]{1,0:T(8,128)} %depth_ref.1, f32[16,1024]{1,0:T(8,128)} %press_ref.1), custom_call_target="tpu_custom_call" | custom-call | tf_op jit(solution)/shard_map/wake_step/pallas_call | solution.py:476
  38.4 1.6 %copy.5 = f32[1,2,16,1024]{3,2,1,0:T(8,128)} copy(f32[1,2,16,1024]{3,2,1,0:T(8,128)} %wake_step.1) | data formatting | bytes 262144

commit v3 on v2

--- a/solution.py
+++ b/solution.py
@@ -82,11 +82,24 @@
     return beta
 
 
+def meetings(tiles):
+    bits = [1 << k for k in range((tiles - 1).bit_length())]
+    known = {0, *bits}
+    rounds = []
+    while True:
+        few = known | {1 ^ v for v in known}
+        those = [1] if rounds and len(few) == tiles else bits
+        known = known | {b ^ v for b in those for v in known}
+        rounds.append(those)
+        if len(known) == tiles:
+            return rounds
+
+
 def kernel(
     tiles, slices, rows, state_ref, depth_ref, press_ref, out_ref,
     raw, raw_d, raw_p, x, later, dm, dw, wfac, coarse, total, res, c, u, planes, top, out_c, out_y,
     part, slots, chain, chain_in,
-    load_s, halo_s, halo_r, sum_s, sum_r, chain_s, chain_r,
+    load_s, halo_s, halo_r, sum_s, sum_r, chain_s, chain_r, ready,
 ):
     me = lax.axis_index("tile")
     cut = lax.axis_index("cuts")
@@ -113,10 +126,22 @@
         x[p, :, end : end + PAD] = jnp.zeros((blocks, PAD, LANE), jnp.float32)
 
     barrier = pltpu.get_barrier_semaphore()
-    for d in range(1, tiles):
-        pl.semaphore_signal(
-            barrier, inc=1, device_id={"tile": lax.rem(me + d, tiles)}, device_id_type=MESH
-        )
+    cross = me + 2 * lax.rem(me, 2) - 1
+    has_cross = (cross >= 0) & (cross < tiles)
+
+    def partner(bit):
+        return me + bit * (1 - 2 * lax.rem(me // bit, 2))
+
+    def tell(sem, bits):
+        for bit in bits:
+            pl.semaphore_signal(sem, inc=1, device_id={"tile": partner(bit)}, device_id_type=MESH)
+
+    bits = [1 << k for k in range((tiles - 1).bit_length())]
+    tell(barrier, bits)
+
+    @pl.when(has_cross)
+    def _():
+        pl.semaphore_signal(barrier, inc=1, device_id={"tile": cross}, device_id_type=MESH)
 
     @pl.when(has_prev)
     def _():
@@ -190,9 +215,19 @@
         columns(a)
 
     pl.semaphore_wait(
-        barrier, tiles - 1 + has_prev.astype(jnp.int32) + has_next.astype(jnp.int32)
+        barrier,
+        len(bits)
+        + has_cross.astype(jnp.int32)
+        + has_prev.astype(jnp.int32)
+        + has_next.astype(jnp.int32),
     )
-    halo_both([0], start)
+    rounds = meetings(tiles)
+    for k, those in enumerate(rounds):
+        tell(ready.at[k], those)
+        if k == 0:
+            halo_both([0], start)
+        if k < len(rounds) - 1:
+            pl.semaphore_wait(ready.at[k], len(those))
     halo_both(NEAR_PARTS, start)
 
     depth = x[1, :, PAD:end]
@@ -358,6 +393,8 @@
 
     for s in range(STAGES):
         inner_products(s)
+        if s == 0:
+            pl.semaphore_wait(ready.at[len(rounds) - 1], len(rounds[-1]))
         for d in range(1, tiles):
             sum_copy(s, d).start()
         own_tops()
@@ -507,6 +544,7 @@
             pltpu.SemaphoreType.DMA((STAGES, tiles)),
             pltpu.SemaphoreType.DMA((pieces,)),
             pltpu.SemaphoreType.DMA((pieces,)),
+            pltpu.SemaphoreType.REGULAR((len(meetings(tiles)),)),
         ],
         compiler_params=pltpu.CompilerParams(
             collective_id=0, has_side_effects=True, vmem_limit_bytes=60 * 1024 * 1024

time: 40.1 us -> 38.8 us (0.968)
  Pallas kernels: 38.3 us -> 37 us
    pallas_call x1, Pallas kernels: 38.3 us -> 37 us  [local(): pl.pallas_call(functools.partial(kernel, tiles, slices, rows), out_shape=...]
where the time goes in v3:
time: 38.8 us; the launch traced here: 38.6 us
  Pallas kernels  37 us (95%)
  local copies, waits for them, and re-layouts  1.57 us (4%)
    pallas_call x1, Pallas kernels, local(): pl.pallas_call(functools.partial(kernel, tiles, slices, rows), out_shape=...  37 us
    unnamed x1, local copies, waits for them, and re-layouts  1.57 us

profile of v3, /device:TPU:3, one launch (start us, length us, event | category | flops | bytes accessed | tf_op | source)
XLA Modules:
  0.0 38.6 jit_solution(13358821040682910821)
XLA Ops:
  0.0 37.0 %wake_step.1 = f32[1,2,16,1024]{3,2,1,0:T(8,128)} custom-call(f32[1,2,16,1024]{3,2,1,0:T(8,128)} %state_ref.1, f32[16,1024]{1,0:T(8,128)} %depth_ref.1, f32[16,1024]{1,0:T(8,128)} %press_ref.1), custom_call_target="tpu_custom_call" | custom-call | tf_op jit(solution)/shard_map/wake_step/pallas_call | solution.py:513
  37.1 1.6 %copy.5 = f32[1,2,16,1024]{3,2,1,0:T(8,128)} copy(f32[1,2,16,1024]{3,2,1,0:T(8,128)} %wake_step.1) | data formatting | bytes 262144

commit v4 on v3

--- a/solution.py
+++ b/solution.py
@@ -19,6 +19,7 @@
 FOLD = 5
 PAD = 16
 SPAN = 24
+GROUP = 2
 PARTS = [(0, 2, 0, 4), (0, 2, 4, 3), (2, 2, 0, 5), (0, 2, 7, 6), (2, 2, 5, 6)]
 NEAR_PARTS = [1, 2]
 FAR_PARTS = [3, 4]
@@ -37,6 +38,30 @@
     before = jnp.where(lane == 0, jnp.concatenate([zero, r[:-1]], axis=0), r)
     after = jnp.where(lane == LANE - 1, jnp.concatenate([l[1:], zero], axis=0), l)
     return before, after
+
+
+def stream(ref, a):
+    lane = lax.broadcasted_iota(jnp.int32, (SUB, LANE), 1)
+    blocks = ref.shape[0]
+    r_old = l_old = r_far = None
+    for j in range(blocks + 1):
+        if j < blocks:
+            v = ref[j, a : a + SUB]
+            r = pltpu.roll(v, 1, axis=1)
+            l = pltpu.roll(v, LANE - 1, axis=1)
+        else:
+            l = jnp.zeros((SUB, LANE), jnp.float32)
+        if j > 0:
+            before = jnp.where(lane == 0, r_far, r_old)
+            after = jnp.where(lane == LANE - 1, l, l_old)
+            yield j - 1, before, after
+        r_far = r_old if j > 0 else jnp.zeros((SUB, LANE), jnp.float32)
+        r_old, l_old = r, l
+
+
+def all_around(ref, a):
+    for j, before, after in stream(ref, a):
+        yield j, (ref[j, a + 1 : a + 1 + SUB] + ref[j, a - 1 : a - 1 + SUB]) + (before + after)
 
 
 def rows8(ref, a):
@@ -97,7 +122,7 @@
 
 def kernel(
     tiles, slices, rows, state_ref, depth_ref, press_ref, out_ref,
-    raw, raw_d, raw_p, x, later, dm, dw, wfac, coarse, total, res, c, u, planes, top, out_c, out_y,
+    raw, raw_d, raw_p, x, later, dm, dw, dw_before, dw_after, first_top, wfac, coarse, total, res, beside, sides_ref, c, u, top, out_c, out_y,
     part, slots, chain, chain_in,
     load_s, halo_s, halo_r, sum_s, sum_r, chain_s, chain_r, ready,
 ):
@@ -121,22 +146,19 @@
     for load in loads:
         load.start()
 
-    for p in range(4):
-        x[p, :, 0:PAD] = jnp.zeros((blocks, PAD, LANE), jnp.float32)
-        x[p, :, end : end + PAD] = jnp.zeros((blocks, PAD, LANE), jnp.float32)
-
     barrier = pltpu.get_barrier_semaphore()
     cross = me + 2 * lax.rem(me, 2) - 1
     has_cross = (cross >= 0) & (cross < tiles)
 
-    def partner(bit):
-        return me + bit * (1 - 2 * lax.rem(me // bit, 2))
+    bits = [1 << k for k in range((tiles - 1).bit_length())]
+
+    def partner(d):
+        return me + sum(bit * (1 - 2 * lax.rem(me // bit, 2)) for bit in bits if d & bit)
 
     def tell(sem, bits):
         for bit in bits:
             pl.semaphore_signal(sem, inc=1, device_id={"tile": partner(bit)}, device_id_type=MESH)
 
-    bits = [1 << k for k in range((tiles - 1).bit_length())]
     tell(barrier, bits)
 
     @pl.when(has_cross)
@@ -150,6 +172,12 @@
     @pl.when(has_next)
     def _():
         pl.semaphore_signal(barrier, inc=1, device_id={"cuts": cut + 1}, device_id_type=MESH)
+
+    for there, a in ((has_lo, 0), (has_hi, end)):
+
+        @pl.when(jnp.logical_not(there))
+        def _():
+            x[:, :, a : a + PAD] = jnp.zeros((4, blocks, PAD, LANE), jnp.float32)
 
     for load in loads:
         load.wait()
@@ -197,12 +225,16 @@
         inv_depth = 1.0 / safe
         vert = LEVELS * inv_depth
         vert = vert * vert
+        tops = None
         for m in range(LEVELS):
             inverse = 1.0 / (vert * LAM[m] - 4.0)
             if inside is not None:
                 inverse = jnp.where(inside, inverse, 0.0)
             dm[m, :, a : a + SUB] = inverse
             dw[m, :, a : a + SUB] = WEIGHT[m] * inverse
+            t = (TOPROW[m] * WEIGHT[m]) * inverse
+            tops = t if tops is None else tops + t
+        first_top[:, a : a + SUB] = tops
         wfac[:, a : a + SUB] = (0.5 * LEVELS) * inv_depth
 
     sub = lax.broadcasted_iota(jnp.int32, (1, SUB, LANE), 1)
@@ -210,9 +242,6 @@
     def edge_columns(a_lo, own_lo, a_hi, own_hi):
         columns(a_lo, sub + SUB * has_lo.astype(jnp.int32) >= own_lo)
         columns(a_hi, sub - SUB * has_hi.astype(jnp.int32) < own_hi)
-
-    for a in own:
-        columns(a)
 
     pl.semaphore_wait(
         barrier,
@@ -222,14 +251,11 @@
         + has_next.astype(jnp.int32),
     )
     rounds = meetings(tiles)
-    for k, those in enumerate(rounds):
-        tell(ready.at[k], those)
-        if k == 0:
-            halo_both([0], start)
-        if k < len(rounds) - 1:
-            pl.semaphore_wait(ready.at[k], len(those))
-    halo_both(NEAR_PARTS, start)
-
+    tell(ready.at[0], rounds[0])
+    halo_both([0], start)
+
+    for a in own:
+        columns(a)
     depth = x[1, :, PAD:end]
     stiff = jnp.tanh(depth)
     z = TIME_STEP * TIME_STEP * stiff
@@ -240,6 +266,11 @@
     coarse[1] = stiff * sine
     coarse[2] = -sine
 
+    for k in range(1, len(rounds)):
+        pl.semaphore_wait(ready.at[k - 1], len(rounds[k - 1]))
+        tell(ready.at[k], rounds[k])
+    halo_both(NEAR_PARTS, start)
+
     halo_both([0], arrive)
     edge_columns(PAD - 4, 4, end - 4, 4)
 
@@ -249,7 +280,7 @@
             dst_ref=slots.at[s, d],
             send_sem=sum_s.at[s, d],
             recv_sem=sum_r.at[s, d],
-            device_id={"tile": lax.rem(me + d, tiles)},
+            device_id={"tile": partner(d)},
             device_id_type=MESH,
         )
 
@@ -265,47 +296,89 @@
         phi = phi_of(s)
         for a in wide:
             res[:, a : a + SUB] = 4.0 * rows8(phi, a) - neighbours(phi, a)
-        gram = [None] * 9
+        if s == 0:
+            for a in wide:
+                r = rows8(res, a)
+                for m in range(LEVELS):
+                    c[m, 0, :, a : a + SUB] = rows8(dw.at[m], a) * r
+        else:
+            for a in wide:
+                for j, before, after in stream(res, a):
+                    beside[0, j, a : a + SUB] = before
+                    beside[1, j, a : a + SUB] = after
+        gram = [None] * 10
 
         def add(k, v):
             gram[k] = v if gram[k] is None else gram[k] + v
 
-        for a in wide:
-            r = rows8(res, a)
-            for m in range(LEVELS):
-                c[m, 0, :, a : a + SUB] = rows8(dw.at[m], a) * r
-        for i in range(2):
-            for m in range(LEVELS):
-                for a in wide:
-                    v = neighbours(c.at[m, i], a)
-                    u[m, i, :, a : a + SUB] = v
-                    c[m, i + 1, :, a : a + SUB] = rows8(dm.at[m], a) * v
-        for m in range(LEVELS):
-            for a in own:
-                us = [rows8(res, a), rows8(u.at[m, 0], a), rows8(u.at[m, 1], a), neighbours(c.at[m, 2], a)]
-                k = 0
-                for i in range(4):
-                    for j in range(max(i, 1), 4):
-                        v = jnp.sum(us[i] * us[j], axis=0)
-                        add(k, WEIGHT[m] * v if i == 0 else v)
+        def first_power(ms, a, j):
+            at, up, down = slice(a, a + SUB), slice(a + 1, a + 1 + SUB), slice(a - 1, a - 1 + SUB)
+            r_up, r_down = res[j, up], res[j, down]
+            before, after = beside[0, j, at], beside[1, j, at]
+            for m in ms:
+                v = (dw[m, j, up] * r_up + dw[m, j, down] * r_down) + (
+                    dw_before[m, j, at] * before + dw_after[m, j, at] * after
+                )
+                u[m, 0, j, at] = v
+                c[m, 1, j, at] = dm[m, j, at] * v
+
+        def power(i, m, a):
+            at = slice(a, a + SUB)
+            for j, v in all_around(c.at[m, i], a):
+                u[m, i, j, at] = v
+                if i < 2:
+                    c[m, i + 1, j, at] = dm[m, j, at] * v
+
+        def products(ms, a, j):
+            at = slice(a, a + SUB)
+            if ms[0] == 0:
+                sides = [None] * 6
+            else:
+                sides = [sides_ref[i, j, at] for i in range(6)]
+            for m in ms:
+                us = [u[m, i, j, at] for i in range(3)]
+                k = 4
+                for p in range(3):
+                    for q in range(p, 3):
+                        add(k, us[p] * us[q])
                         k += 1
-                for i in range(3):
-                    if m == 0:
-                        planes[i, :, a : a + SUB] = us[i + 1]
-                    else:
-                        planes[i, :, a : a + SUB] += us[i + 1]
-        gram = [4.0 * g for g in gram]
-        square = None
-        for a in own:
-            bottom = [rows8(res, a)] + [rows8(planes.at[i], a) for i in range(3)]
-            k = 0
-            for i in range(4):
-                for j in range(max(i, 1), 4):
-                    gram[k] = gram[k] + 0.5 * jnp.sum(bottom[i] * bottom[j], axis=0)
+                    w = WEIGHT[m] * us[p]
+                    sides[p] = us[p] if m == 0 else sides[p] + us[p]
+                    sides[3 + p] = w if m == 0 else sides[3 + p] + w
+            if ms[-1] < LEVELS - 1:
+                for i in range(6):
+                    sides_ref[i, j, at] = sides[i]
+                return
+            u0 = res[j, at]
+            add(0, u0 * u0)
+            k = 4
+            for p in range(3):
+                add(1 + p, u0 * (sides[3 + p] + 0.125 * sides[p]))
+                part_p = 0.125 * sides[p]
+                for q in range(p, 3):
+                    add(k, part_p * sides[q])
                     k += 1
-            v = jnp.sum(bottom[0] * bottom[0], axis=0)
-            square = v if square is None else square + v
-        gram = [jnp.sum(g, axis=0, keepdims=True) for g in [LEVELS * square] + gram]
+
+        groups = [list(range(m, m + GROUP)) for m in range(0, LEVELS, GROUP)]
+
+        def work(kind, ms):
+            if kind == 0 and s > 0:
+                return [functools.partial(first_power, ms, a, j) for a in wide for j in range(blocks)]
+            if kind < 3:
+                windows = own if kind == 2 else wide
+                return [functools.partial(power, kind, m, a) for m in ms for a in windows]
+            return [functools.partial(products, ms, a, j) for a in own for j in range(blocks)]
+
+        for step in range(len(groups) + 3):
+            tasks = []
+            for kind in range(4):
+                if 0 <= step - kind < len(groups):
+                    todo = work(kind, groups[step - kind])
+                    tasks += [((n + 0.5) / len(todo), kind, n, task) for n, task in enumerate(todo)]
+            for _, _, _, task in sorted(tasks, key=lambda entry: entry[:3]):
+                task()
+        gram = [LEVELS * gram[0]] + [4.0 * g for g in gram[1:]]
+        gram = [jnp.sum(g, axis=0, keepdims=True) for g in gram]
         for k in range(FOLD):
             a, b = gram[k], gram[k + FOLD]
             part[s, k : k + 1] = jnp.where(half, a, b) + pltpu.roll(
@@ -314,7 +387,8 @@
 
     def own_tops():
         for a in own:
-            for i in range(3):
+            top[0, :, a : a + SUB] = rows8(first_top, a) * rows8(res, a)
+            for i in range(1, 3):
                 y = None
                 for m in range(LEVELS):
                     v = TOPROW[m] * rows8(c.at[m, i], a)
@@ -395,7 +469,7 @@
         inner_products(s)
         if s == 0:
             pl.semaphore_wait(ready.at[len(rounds) - 1], len(rounds[-1]))
-        for d in range(1, tiles):
+        for d in range(tiles - 1, 0, -1):
             sum_copy(s, d).start()
         own_tops()
         known = [explicit(s, a) for a in own] if s > 0 else None
@@ -404,6 +478,11 @@
             halo_both(NEAR_PARTS, arrive)
             edge_columns(PAD - 7, 7, end - 1, 1)
             known = [explicit(s, a) for a in own]
+            for m in range(LEVELS):
+                for a in wide:
+                    before, after = rolled(rows8(dw.at[m], a))
+                    dw_before[m, :, a : a + SUB] = before
+                    dw_after[m, :, a : a + SUB] = after
         if s == 1:
             halo_both(FAR_PARTS, arrive)
             edge_columns(PAD - 13, SUB, end + 5, 0)
@@ -523,13 +602,17 @@
             pltpu.VMEM((STAGES - 1, 2) + field, f32),
             pltpu.VMEM((LEVELS,) + field, f32),
             pltpu.VMEM((LEVELS,) + field, f32),
+            pltpu.VMEM((LEVELS,) + field, f32),
+            pltpu.VMEM((LEVELS,) + field, f32),
+            pltpu.VMEM(field, f32),
             pltpu.VMEM(field, f32),
             pltpu.VMEM((3,) + plane, f32),
             pltpu.VMEM((2,) + plane, f32),
             pltpu.VMEM(field, f32),
+            pltpu.VMEM((2,) + field, f32),
+            pltpu.VMEM((6,) + field, f32),
             pltpu.VMEM((LEVELS, 3) + field, f32),
-            pltpu.VMEM((LEVELS, 2) + field, f32),
-            pltpu.VMEM((3,) + field, f32),
+            pltpu.VMEM((LEVELS, 3) + field, f32),
             pltpu.VMEM((3,) + field, f32),
             pltpu.VMEM((LEVELS, 2, 2, blocks, SPAN, LANE), f32),
             pltpu.VMEM((2, 3, blocks, SUB, LANE), f32),

time: 38.8 us -> 38.4 us (0.990)
  no operation moved by 1% of the time
where the time goes in v4:
time: 38.4 us; the launch traced here: 38.3 us
  Pallas kernels  36.7 us (96%)
  local copies, waits for them, and re-layouts  1.57 us (4%)
    pallas_call x1, Pallas kernels, local(): pl.pallas_call(functools.partial(kernel, tiles, slices, rows), out_shape=...  36.7 us
    unnamed x1, local copies, waits for them, and re-layouts  1.57 us

profile of v4, /device:TPU:3, one launch (start us, length us, event | category | flops | bytes accessed | tf_op | source)
XLA Modules:
  0.0 38.3 jit_solution(16895163454406456754)
XLA Ops:
  0.0 36.7 %wake_step.1 = f32[1,2,16,1024]{3,2,1,0:T(8,128)} custom-call(f32[1,2,16,1024]{3,2,1,0:T(8,128)} %state_ref.1, f32[16,1024]{1,0:T(8,128)} %depth_ref.1, f32[16,1024]{1,0:T(8,128)} %press_ref.1), custom_call_target="tpu_custom_call" | custom-call | tf_op jit(solution)/shard_map/wake_step/pallas_call | solution.py:592
  36.7 1.6 %copy.5 = f32[1,2,16,1024]{3,2,1,0:T(8,128)} copy(f32[1,2,16,1024]{3,2,1,0:T(8,128)} %wake_step.1) | data formatting | bytes 262144

commit v5 on v4

--- a/solution.py
+++ b/solution.py
@@ -277,9 +277,9 @@
     def sum_copy(s, d):
         return pltpu.make_async_remote_copy(
             src_ref=part.at[s],
-            dst_ref=slots.at[s, d],
-            send_sem=sum_s.at[s, d],
-            recv_sem=sum_r.at[s, d],
+            dst_ref=slots.at[s % 2, d - 1],
+            send_sem=sum_s.at[s % 2, d - 1],
+            recv_sem=sum_r.at[s % 2, d - 1],
             device_id={"tile": partner(d)},
             device_id_type=MESH,
         )
@@ -471,6 +471,11 @@
             pl.semaphore_wait(ready.at[len(rounds) - 1], len(rounds[-1]))
         for d in range(tiles - 1, 0, -1):
             sum_copy(s, d).start()
+        if s > 0:
+            for d in range(1, tiles):
+                sum_copy(s - 1, d).wait_send()
+        if s == STAGES - 1:
+            halo_both(range(len(PARTS)), leave)
         own_tops()
         known = [explicit(s, a) for a in own] if s > 0 else None
         if s == 0:
@@ -501,7 +506,7 @@
             sum_copy(s, d).wait_recv()
         whole = part[s]
         for d in range(1, tiles):
-            whole = whole + slots[s, d]
+            whole = whole + slots[s % 2, d - 1]
         low = jnp.sum(jnp.where(half, whole, 0.0), axis=1, keepdims=True)
         high = jnp.sum(jnp.where(half, 0.0, whole), axis=1, keepdims=True)
         sums = [low[k : k + 1] for k in range(FOLD)] + [high[k : k + 1] for k in range(FOLD)]
@@ -570,16 +575,13 @@
         for k in range(2):
             out_ref[0, k, :, j * LANE : (j + 1) * LANE] = chain[j, k]
 
-    halo_both(range(len(PARTS)), leave)
-
     @pl.when(has_next)
     def _():
         for k in range(len(pieces)):
             chain_copy(k).wait_send()
 
-    for s in range(STAGES):
-        for d in range(1, tiles):
-            sum_copy(s, d).wait_send()
+    for d in range(1, tiles):
+        sum_copy(STAGES - 1, d).wait_send()
 
 
 def local(tiles, slices, state_in, sea_depth, pressure):
@@ -617,14 +619,14 @@
             pltpu.VMEM((LEVELS, 2, 2, blocks, SPAN, LANE), f32),
             pltpu.VMEM((2, 3, blocks, SUB, LANE), f32),
             pltpu.VMEM((STAGES, FOLD, LANE), f32),
-            pltpu.VMEM((STAGES, tiles, FOLD, LANE), f32),
+            pltpu.VMEM((2, tiles - 1, FOLD, LANE), f32),
             pltpu.VMEM((blocks, 2, rows, LANE), f32),
             pltpu.VMEM((blocks, 2, rows, LANE), f32),
             pltpu.SemaphoreType.DMA((3,)),
             pltpu.SemaphoreType.DMA((len(PARTS), 2)),
             pltpu.SemaphoreType.DMA((len(PARTS), 2)),
-            pltpu.SemaphoreType.DMA((STAGES, tiles)),
-            pltpu.SemaphoreType.DMA((STAGES, tiles)),
+            pltpu.SemaphoreType.DMA((2, tiles - 1)),
+            pltpu.SemaphoreType.DMA((2, tiles - 1)),
             pltpu.SemaphoreType.DMA((pieces,)),
             pltpu.SemaphoreType.DMA((pieces,)),
             pltpu.SemaphoreType.REGULAR((len(meetings(tiles)),)),

time: 38.4 us -> 38.1 us (level)
  no operation moved by 1% of the time
where the time goes in v5:
time: 38.1 us; the launch traced here: 38 us
  Pallas kernels  36.4 us (96%)
  local copies, waits for them, and re-layouts  1.57 us (4%)
    pallas_call x1, Pallas kernels, local(): pl.pallas_call(functools.partial(kernel, tiles, slices, rows), out_shape=...  36.4 us
    unnamed x1, local copies, waits for them, and re-layouts  1.57 us

profile of v5, /device:TPU:3, one launch (start us, length us, event | category | flops | bytes accessed | tf_op | source)
XLA Modules:
  0.0 38.0 jit_solution(14731165440521165630)
XLA Ops:
  0.0 36.4 %wake_step.1 = f32[1,2,16,1024]{3,2,1,0:T(8,128)} custom-call(f32[1,2,16,1024]{3,2,1,0:T(8,128)} %state_ref.1, f32[16,1024]{1,0:T(8,128)} %depth_ref.1, f32[16,1024]{1,0:T(8,128)} %press_ref.1), custom_call_target="tpu_custom_call" | custom-call | tf_op jit(solution)/shard_map/wake_step/pallas_call | solution.py:594
  36.4 1.6 %copy.5 = f32[1,2,16,1024]{3,2,1,0:T(8,128)} copy(f32[1,2,16,1024]{3,2,1,0:T(8,128)} %wake_step.1) | data formatting | bytes 262144

commit v6 on v5

--- a/solution.py
+++ b/solution.py
@@ -19,7 +19,7 @@
 FOLD = 5
 PAD = 16
 SPAN = 24
-GROUP = 2
+GROUP = 4
 PARTS = [(0, 2, 0, 4), (0, 2, 4, 3), (2, 2, 0, 5), (0, 2, 7, 6), (2, 2, 5, 6)]
 NEAR_PARTS = [1, 2]
 FAR_PARTS = [3, 4]
@@ -571,9 +571,9 @@
         def _():
             chain_copy(k).start()
 
-    for j in range(blocks):
-        for k in range(2):
-            out_ref[0, k, :, j * LANE : (j + 1) * LANE] = chain[j, k]
+        for j in range(first, first + chunk):
+            for i in range(2):
+                out_ref[0, i, :, j * LANE : (j + 1) * LANE] = chain[j, i]
 
     @pl.when(has_next)
     def _():

time: 38.1 us -> 38.1 us (level)
  no operation moved by 1% of the time
where the time goes in v6:
time: 38.1 us; the launch traced here: 38 us
  Pallas kernels  36.4 us (96%)
  local copies, waits for them, and re-layouts  1.57 us (4%)
    pallas_call x1, Pallas kernels, local(): pl.pallas_call(functools.partial(kernel, tiles, slices, rows), out_shape=...  36.4 us
    unnamed x1, local copies, waits for them, and re-layouts  1.57 us

profile of v6, /device:TPU:3, one launch (start us, length us, event | category | flops | bytes accessed | tf_op | source)
XLA Modules:
  0.0 38.0 jit_solution(1693836762065862601)
XLA Ops:
  0.0 36.4 %wake_step.1 = f32[1,2,16,1024]{3,2,1,0:T(8,128)} custom-call(f32[1,2,16,1024]{3,2,1,0:T(8,128)} %state_ref.1, f32[16,1024]{1,0:T(8,128)} %depth_ref.1, f32[16,1024]{1,0:T(8,128)} %press_ref.1), custom_call_target="tpu_custom_call" | custom-call | tf_op jit(solution)/shard_map/wake_step/pallas_call | solution.py:594
  36.4 1.6 %copy.5 = f32[1,2,16,1024]{3,2,1,0:T(8,128)} copy(f32[1,2,16,1024]{3,2,1,0:T(8,128)} %wake_step.1) | data formatting | bytes 262144
